TPU v7x, 512 devices: a whole 4x4x16 slice. The times are simulated.
512 devices in a mesh: dp: 2 (over y_lo), ctx: 64 (over z, y_hi, core), tp: 4 (over x).
Axes of the slice: x: 4, y: 4 (y_hi: 2, y_lo: 2; y = y_hi * 2 + y_lo), z: 16, core: 2. Of those that a mesh axis runs over, the one named last changes fastest.
Arguments:
- values: bfloat16 [2, 8192, 4096], P('dp', 'ctx', 'tp'), may hold values from -6 to 6
- gate_input: bfloat16 [2, 8192, 4096], P('dp', 'ctx', 'tp'), may hold values from -6 to 6
- filter_param: bfloat16 [8192, 4096], P('ctx', 'tp'), may hold values from -6 to 6
- grad_y: bfloat16 [2, 8192, 4096], P('dp', 'ctx', 'tp'), may hold values from -6 to 6
Outputs:
- grad_gate: bfloat16 [2, 8192, 4096], P('dp', 'ctx', 'tp')
- grad_values: bfloat16 [2, 8192, 4096], P('dp', 'ctx', 'tp')
- grad_filter: float32 [8192, 4096], P('ctx', 'tp')
All inputs are finite; a program needn't handle non-finite values.
Results may differ from a plain program's by a relative error of at most 0.01.
Values may be sent and summed in bfloat16 or wider, within the bound.
A program may use at most 64 MiB of HBM per device.

v0:
```python
import math

import jax
import jax.numpy as jnp
from jax import lax
from jax.sharding import PartitionSpec as P

PRECISE = lax.Precision.HIGHEST


def angle_pair(index_table, period):
    angles = (index_table % period).astype(jnp.float32) * (2.0 * math.pi / period)
    return (jnp.cos(angles), jnp.sin(angles))


def circle(left_index, right_index, period):
    return angle_pair(left_index[:, None] * right_index[None, :], period)


def body(values, gate_input, filter_param, grad_y):
    ctx_count = lax.axis_size("ctx")
    local_len = values.shape[1]
    pieces = local_len // ctx_count
    chan_count = values.shape[2]
    total_len = local_len * ctx_count
    padded = 2 * total_len
    inv_root = 1.0 / math.sqrt(total_len)
    inv_total = 1.0 / padded
    my_rank = lax.axis_index("ctx")
    grad_rows = grad_y[0].astype(jnp.float32)
    grad_s = (grad_rows * gate_input[0].astype(jnp.float32)).astype(jnp.bfloat16)
    stacked = jnp.stack([values[0], filter_param, grad_s]).reshape(3, ctx_count, pieces, chan_count)
    by_piece = lax.all_to_all(stacked, "ctx", split_axis=1, concat_axis=1, tiled=True)
    piece_data = by_piece.astype(jnp.float32)
    q_index = jnp.arange(ctx_count, dtype=jnp.int32)
    k_order = jnp.arange(2 * ctx_count, dtype=jnp.int32)
    r_inner = my_rank * pieces + jnp.arange(pieces, dtype=jnp.int32)
    positions = q_index[:, None] * local_len + r_inner[None, :]
    cos_one, sin_one = angle_pair(k_order[:, None, None] * positions[None], padded)
    table_one = jnp.stack([cos_one, -sin_one])
    first = jnp.einsum("okqr,sqrc->oskrc", table_one, piece_data, precision=PRECISE)
    by_freq = lax.all_to_all(first, "ctx", split_axis=2, concat_axis=3, tiled=True)
    r_all = jnp.arange(local_len, dtype=jnp.int32)
    cos_row, sin_row = circle(r_all, r_all, local_len)
    table_two = jnp.stack(
        [jnp.stack([cos_row, sin_row], axis=1), jnp.stack([-sin_row, cos_row], axis=1)]
    )
    spec = jnp.einsum("okir,isjrc->osjkc", table_two, by_freq, precision=PRECISE)
    spec_re = spec[0]
    spec_im = spec[1]
    val_re, val_im = (spec_re[0], spec_im[0])
    grad_re, grad_im = (spec_re[2], spec_im[2])
    filt_re, filt_im = (spec_re[1] * inv_root, spec_im[1] * inv_root)
    conv_re = val_re * filt_re - val_im * filt_im
    conv_im = val_re * filt_im + val_im * filt_re
    back_re = grad_re * filt_re + grad_im * filt_im
    back_im = grad_im * filt_re - grad_re * filt_im
    cross_re = (grad_re * val_re + grad_im * val_im) * inv_root
    cross_im = (grad_im * val_re - grad_re * val_im) * inv_root
    inverse_in = jnp.stack(
        [jnp.stack([conv_re, back_re, cross_re]), jnp.stack([conv_im, back_im, cross_im])]
    )
    k_local = lax.dynamic_slice_in_dim(k_order, 2 * my_rank, 2)
    k_full = r_all[None, :] * (2 * ctx_count) + k_local[:, None]
    cos_three, sin_three = angle_pair(r_all[None, :, None] * k_full[:, None, :], padded)
    table_three = jnp.stack(
        [jnp.stack([cos_three, -sin_three], axis=2), jnp.stack([sin_three, cos_three], axis=2)]
    )
    rotated = jnp.einsum("ojrik,isjkc->osjrc", table_three, inverse_in, precision=PRECISE)
    gathered = lax.all_to_all(rotated, "ctx", split_axis=3, concat_axis=2, tiled=True)
    cos_last, sin_last = circle(q_index, k_order, 2 * ctx_count)
    table_four = jnp.stack([cos_last, -sin_last], axis=2) * inv_total
    row_blocks = jnp.einsum("qki,iskrc->sqrc", table_four, gathered, precision=PRECISE)
    result = lax.all_to_all(row_blocks, "ctx", split_axis=1, concat_axis=2, tiled=True)
    conv_out = result[0, 0]
    grad_values = result[1, 0]
    grad_filter = lax.psum(result[2, 0].astype(jnp.bfloat16), "dp").astype(jnp.float32)
    grad_gate = (grad_rows * conv_out).astype(jnp.bfloat16)
    return (grad_gate[None], grad_values.astype(jnp.bfloat16)[None], grad_filter)


def solution(mesh):
    placed = (P("dp", "ctx", "tp"), P("dp", "ctx", "tp"), P("ctx", "tp"), P("dp", "ctx", "tp"))
    return jax.shard_map(
        body,
        mesh=mesh,
        in_specs=placed,
        out_specs=(P("dp", "ctx", "tp"), P("dp", "ctx", "tp"), P("ctx", "tp")),
        check_vma=False,
    )
```

profile of v0, /device:TPU:1, one launch (start us, length us, event | category | flops | bytes accessed | tf_op | source)
XLA Modules:
  0.0 862.2 jit_solution(4931563284041388915)
XLA Ops:
  7.2 1.0 stack.80
  8.2 2.6 fusion.29
  10.9 1.1 stack.81
  12.0 1.3 pad_maximum_fusion
  13.3 1.4 copy.77
  14.8 19.8 %all-to-all-start = ((bf16[3,64,2,1024]{3,2,0,1:T(2,128)(2,1)}), bf16[3,64,2,1024]{3,2,0,1:T(2,128)(2,1)S(1)}, u32[]{:S(2)}, u32[]{:S(2)}) async-start(bf16[3,64,2,1024]{3,2,0,1:T(2,128)(2,1)} %copy.77), calls=%async_computation | async-start | bytes 1572864 | tf_op jit(solution)/shard_map/all_to_all | solution.py:33
  35.0 43.1 %all-to-all-done = bf16[3,64,2,1024]{3,2,0,1:T(2,128)(2,1)S(1)} async-done(((bf16[3,64,2,1024]{3,2,0,1:T(2,128)(2,1)}), bf16[3,64,2,1024]{3,2,0,1:T(2,128)(2,1)S(1)}, u32[]{:S(2)}, u32[]{:S(2)}) %all-to-all-start) | async-done | bytes 786464 | tf_op jit(solution)/shard_map/all_to_all | solution.py:33
  78.1 4.5 convolution_bitcast_fusion
  82.6 10.4 %copy.79 = f32[2,3,128,2,1024]{4,0,1,3,2:T(2,128)} copy(f32[2,3,128,2,1024]{2,4,0,1,3:T(8,128)} %convolution_bitcast_fusion) | data formatting | bytes 12582912 | tf_op jit(solution)/shard_map/okqr,sqrc->oskrc/transpose | solution.py:41
  93.0 7.3 all-to-all-start.1
  101.0 0.7 maximum_bitcast_fusion.11
  102.2 0.7 maximum_bitcast_fusion.7
  103.0 269.1 %all-to-all-done.1 = f32[2,3,128,2,1024]{4,0,1,3,2:T(2,128)} async-done(((f32[2,3,128,2,1024]{4,0,1,3,2:T(2,128)}), f32[2,3,128,2,1024]{4,0,1,3,2:T(2,128)}, u32[]{:S(2)}, u32[]{:S(2)}) %all-to-all-start.1) | async-done | bytes 6291488 | tf_op jit(solution)/shard_map/all_to_all | solution.py:42
  372.1 7.6 copy.81
  379.8 12.5 %fusion.4 = f32[2,3,2,128,1024]{3,4,0,2,1:T(8,128)S(1)} fusion(f32[2,3,2,128,1024,1]{4,2,3,1,0,5:T(2,128)S(1)} %bitcast.174, f32[1,128,2,128]{3,1,2,0:T(8,128)} %get-tuple-element.21, f32[1,128,2,128]{3,1,2,0:T(8,128)S(1)} %get-tuple-element.20), kind=kOutput, calls=%fused_computation.8 | convolution fusion | flops 4831903744 | bytes 12845056 | tf_op jit(solution)/shard_map/okir,isjrc->osjkc/dot_general | solution.py:48
  394.3 7.0 fusion.7
  401.2 10.4 %copy.96 = f32[2,3,2,128,1024]{4,0,1,2,3:T(2,128)} copy(f32[2,3,2,128,1024]{3,4,0,1,2:T(8,128)} %fusion.7) | data formatting | bytes 12582912 | tf_op jit(solution)/shard_map/ojrik,isjkc->osjrc/transpose | solution.py:69
  411.6 14.2 %all-to-all-start.2 = ((f32[2,3,2,128,1024]{4,0,1,2,3:T(2,128)}), f32[2,3,2,128,1024]{4,0,1,2,3:T(2,128)}, u32[]{:S(2)}, u32[]{:S(2)}) async-start(f32[2,3,2,128,1024]{4,0,1,2,3:T(2,128)} %copy.96), calls=%async_computation.2 | async-start | bytes 12582912 | tf_op jit(solution)/shard_map/all_to_all | solution.py:70
  426.2 271.9 %all-to-all-done.2 = f32[2,3,2,128,1024]{4,0,1,2,3:T(2,128)} async-done(((f32[2,3,2,128,1024]{4,0,1,2,3:T(2,128)}), f32[2,3,2,128,1024]{4,0,1,2,3:T(2,128)}, u32[]{:S(2)}, u32[]{:S(2)}) %all-to-all-start.2) | async-done | bytes 6291488 | tf_op jit(solution)/shard_map/all_to_all | solution.py:70
  698.0 8.7 %copy.98 = f32[2,3,64,2,2,1024]{5,3,2,0,4,1:T(2,128)} copy(f32[2,3,64,2,2,1024]{5,0,1,3,4,2:T(2,128)} %bitcast.42) | data formatting | bytes 12582912 | tf_op jit(solution)/shard_map/all_to_all | solution.py:70
  706.7 8.5 all_to_all.44
  715.2 6.2 convolution_bitcast_fusion.1
  721.4 1.2 copy.99
  722.6 90.1 %all_to_all.50 = f32[3,64,2,1024]{3,2,0,1:T(2,128)S(1)} all-to-all(f32[3,64,2,1024]{3,2,0,1:T(2,128)S(1)} %copy.99), channel_id=1, replica_groups=mesh['dp'=2,'ctx'=64,'tp'=4] {'ctx'}, dimensions={1} | all-to-all | bytes 3145728 | tf_op jit(solution)/shard_map/all_to_all | solution.py:74
  812.8 0.5 convert.4
  813.7 0.8 convert_element_type.117
  814.5 0.8 squeeze.2
  815.4 0.5 multiply_convert_fusion
  815.9 0.8 copy.100
  816.7 0.8 convert_element_type.116
  817.5 35.8 %all-reduce.2.cloned.1.call-done = bf16[128,1024]{1,0:T(8,128)(2,1)} async-done(((bf16[128,1024]{1,0:T(8,128)(2,1)}), bf16[128,1024]{1,0:T(8,128)(2,1)}) %all-reduce.2.cloned.1.call-update) | async-done | bytes 262160 | tf_op jit(solution)/shard_map/psum | solution.py:77
  853.3 1.8 convert_element_type.118
  (26 shorter events, 4.4 us)
Async XLA Ops:
  14.8 63.4 %all-to-all-start = ((bf16[3,64,2,1024]{3,2,0,1:T(2,128)(2,1)}), bf16[3,64,2,1024]{3,2,0,1:T(2,128)(2,1)S(1)}, u32[]{:S(2)}, u32[]{:S(2)}) async-start(bf16[3,64,2,1024]{3,2,0,1:T(2,128)(2,1)} %copy.77), calls=%async_computation | async-start | bytes 1572864 | tf_op jit(solution)/shard_map/all_to_all | solution.py:33
  93.0 279.1 %all-to-all-start.1 = ((f32[2,3,128,2,1024]{4,0,1,3,2:T(2,128)}), f32[2,3,128,2,1024]{4,0,1,3,2:T(2,128)}, u32[]{:S(2)}, u32[]{:S(2)}) async-start(f32[2,3,128,2,1024]{4,0,1,3,2:T(2,128)} %copy.79), calls=%async_computation.1 | async-start | bytes 12582912 | tf_op jit(solution)/shard_map/all_to_all | solution.py:42
  393.3 1.0 copy-start.1
  411.6 286.4 %all-to-all-start.2 = ((f32[2,3,2,128,1024]{4,0,1,2,3:T(2,128)}), f32[2,3,2,128,1024]{4,0,1,2,3:T(2,128)}, u32[]{:S(2)}, u32[]{:S(2)}) async-start(f32[2,3,2,128,1024]{4,0,1,2,3:T(2,128)} %copy.96), calls=%async_computation.2 | async-start | bytes 12582912 | tf_op jit(solution)/shard_map/all_to_all | solution.py:70
  425.8 427.6 %all-reduce.2.cloned.1.call-start = ((), (), s32[]{:S(2)}) async-start(), calls=%async_computation.4 | async-start | bytes 524288 | tf_op jit(solution)/shard_map/psum | solution.py:77
  721.4 94.0 %copy-start = (bf16[1,128,1024]{2,1,0:T(8,128)(2,1)S(1)}, bf16[1,128,1024]{2,1,0:T(8,128)(2,1)}, u32[]{:S(2)}) copy-start(bf16[1,128,1024]{2,1,0:T(8,128)(2,1)} %param.7) | copy-start | bytes 786436
Sparse Core Ops, SparseCore 0:
  815.5 37.7 all-reduce.1
where the time goes:
time: 869 us; the launch traced here: 862 us
  waiting for transfers between devices  620 us (71%)
  blocking collectives  90.1 us (10%)
  local copies, waits for them, and re-layouts  54.5 us (6%)
  starting transfers between devices  41.5 us (5%)
  matrix products  30.3 us (3%)
  between operations  14.5 us (2%)
  other arithmetic  11.3 us (1%)
    all_to_all x1, waiting for transfers between devices, body(): lax.all_to_all(rotated, 'ctx', split_axis=3, concat_axis=2, tiled=True)  272 us
    all_to_all x1, waiting for transfers between devices, body(): lax.all_to_all(first, 'ctx', split_axis=2, concat_axis=3, tiled=True)  269 us
    all_to_all x1, blocking collectives, body(): lax.all_to_all(row_blocks, 'ctx', split_axis=1, concat_axis=2, tiled=True)  90.1 us
    all_to_all x1, waiting for transfers between devices, body(): lax.all_to_all(stacked, 'ctx', split_axis=1, concat_axis=1, tiled=True)  43.1 us
    psum x1, waiting for transfers between devices, body(): lax.psum(result[2, 0].astype(jnp.bfloat16), 'dp').astype(jnp.float32)  35.8 us
    all_to_all x1, starting transfers between devices, body(): lax.all_to_all(stacked, 'ctx', split_axis=1, concat_axis=1, tiled=True)  19.8 us
  transfers between devices with their start and end apart: 4, of which 4 were waited for; matrix products, arithmetic and copies ran while one was open for 1% of the time, Pallas kernels for 0%

commit v1 on v0

v1 whole, which is shorter than its diff:
```python
import functools
import math

import jax
import jax.numpy as jnp
import numpy as np
from jax import lax
from jax.experimental import pallas as pl
from jax.experimental.pallas import tpu as pltpu
from jax.sharding import PartitionSpec as P

MESH = pl.DeviceIdType.MESH
F32 = jnp.float32
BF16 = jnp.bfloat16
LANES = 128
GROUP = 4


def make_tables(blocks, width):
    length = blocks * width
    half = blocks // 2
    block_of = np.concatenate([np.arange(half) * 2, np.arange(half) * 2 + 1]).astype(np.float64)
    k1 = np.arange(blocks, dtype=np.float64) + 0.25
    n2 = np.arange(width, dtype=np.float64)
    ang1 = 2.0 * np.pi * k1[:, None] * block_of[None, :] / blocks
    d1 = np.concatenate([np.cos(ang1), -np.sin(ang1)], axis=0)
    d4 = np.concatenate([np.cos(ang1), -np.sin(ang1)], axis=0).T
    ang2 = 2.0 * np.pi * k1[:, None] * n2[None, :] / length
    tw = np.concatenate([np.cos(ang2), np.sin(ang2)], axis=1)
    scale = 1.0 / (length * math.sqrt(length))
    ang3 = 2.0 * np.pi * n2[:, None] * n2[None, :] / width
    co, si = np.cos(ang3), np.sin(ang3)
    fwd = np.block([[co, -si], [si, co]])
    inv = np.block([[co, si], [-si, co]])
    return (
        jnp.asarray(d1, BF16),
        jnp.asarray(d4, BF16),
        jnp.asarray(np.concatenate([tw, tw * scale], axis=1), F32),
        jnp.asarray(fwd, BF16),
        jnp.asarray(inv, BF16),
    )


def kernel(
    blocks,
    v_hbm, gate_hbm, f_hbm, gy_hbm, d1_hbm, d4_hbm, tw_hbm, fwd_hbm, inv_hbm,
    gg_hbm, gv_hbm, gf_hbm,
    in_v, in_gate, in_f, in_gy, d1, d4, tw, fwd, inv,
    s_h, s_v, s_g, r_h, r_v, r_g,
    x32, y32, spec_h, spec_v, spec_g,
    s_c, s_gv, s_gf, r_pair, r_c, r_gv, r_gf,
    o_gg, o_gv, o_gf,
    in_sem, send_sem, recv_sem, out_sem,
):
    chans = in_v.shape[1]
    width = in_v.shape[0]
    ch = chans // blocks
    half = blocks // 2
    rows_half = half * ch
    d = lax.axis_index("dp")
    q = lax.axis_index("ctx")
    core = q % 2
    my_z, my_e = q // 4, q % 4
    zs = blocks // 4
    my_slot = core * half + q // 2

    loads = [
        pltpu.make_async_copy(src, dst, in_sem.at[i])
        for i, (src, dst) in enumerate(
            [
                (f_hbm, in_f), (v_hbm.at[0], in_v), (gy_hbm.at[0], in_gy), (gate_hbm.at[0], in_gate),
                (d1_hbm, d1), (tw_hbm, tw), (fwd_hbm, fwd), (inv_hbm, inv), (d4_hbm, d4),
            ]
        )
    ]
    for load in loads:
        load.start()

    def peer(k):
        step, e = k // 4, k % 4
        dist = (step + 1) // 2
        dz = jnp.where(step % 2 == 1, dist, zs - dist)
        return ((my_z + dz) % zs) * 4 + (my_e + e) % 4

    barrier = pltpu.get_barrier_semaphore()

    def greet(k, carry):
        pl.semaphore_signal(barrier, inc=1, device_id={"ctx": peer(k)}, device_id_type=MESH)
        return carry

    lax.fori_loop(1, blocks, greet, 0)
    pl.semaphore_signal(barrier, inc=1, device_id={"dp": 1 - d}, device_id_type=MESH)

    def rows(ref, start, count):
        return ref.at[pl.ds(pl.multiple_of(start, 16), count), :]

    def wait_bytes(ref, sem):
        pltpu.make_async_copy(ref, ref, sem).wait()

    def transpose_in(block_of, dst):
        for j in range(chans // LANES):
            dst[j * LANES:(j + 1) * LANES, :] = block_of(slice(j * LANES, (j + 1) * LANES)).T.astype(BF16)

    def send_in(src, dst, sem):
        pltpu.make_async_copy(rows(src, q * ch, ch), rows(dst, my_slot * ch, ch), recv_sem.at[sem]).start()

        def one(k, carry):
            to = peer(k)
            pltpu.make_async_remote_copy(
                src_ref=rows(src, to * ch, ch), dst_ref=rows(dst, my_slot * ch, ch),
                send_sem=send_sem.at[sem], recv_sem=recv_sem.at[sem],
                device_id={"ctx": to}, device_id_type=MESH,
            ).start()
            return carry

        lax.fori_loop(1, blocks, one, 0)

    def send_out(src, dst, sem):
        pltpu.make_async_copy(rows(src, my_slot * ch, ch), rows(dst, q * ch, ch), recv_sem.at[sem]).start()

        def one(k, carry):
            to = peer(k)
            slot = (to % 2) * half + to // 2
            pltpu.make_async_remote_copy(
                src_ref=rows(src, slot * ch, ch), dst_ref=rows(dst, q * ch, ch),
                send_sem=send_sem.at[sem], recv_sem=recv_sem.at[sem],
                device_id={"ctx": to}, device_id_type=MESH,
            ).start()
            return carry

        lax.fori_loop(1, blocks, one, 0)

    def pair_copy(src, dst, sem):
        return pltpu.make_async_remote_copy(
            src_ref=src, dst_ref=dst, send_sem=send_sem.at[sem], recv_sem=recv_sem.at[sem],
            device_id={"dp": 1 - d}, device_id_type=MESH,
        )

    H, V, G, HP, CO, GV, GP, GF, GFP = range(9)

    loads[0].wait()
    transpose_in(lambda s: in_f[:, s].astype(F32), s_h)
    pl.semaphore_wait(barrier, blocks)

    @pl.when(core == d)
    def _():
        send_in(s_h, r_h, H)

    loads[1].wait()
    transpose_in(lambda s: in_v[:, s].astype(F32), s_v)
    send_in(s_v, r_v, V)
    loads[2].wait()
    loads[3].wait()
    transpose_in(lambda s: (in_gy[:, s].astype(F32) * in_gate[:, s].astype(F32)).astype(BF16).astype(F32), s_g)
    send_in(s_g, r_g, G)
    for load in loads[4:]:
        load.wait()

    def tw_at(i):
        return tw[:, i * LANES:(i + 1) * LANES]

    def forward(src, spec):
        x32[...] = src[...].astype(F32)
        for g in range(0, ch, GROUP):
            x = jnp.concatenate(
                [x32[pl.ds(c, blocks, stride=ch), :].astype(BF16) for c in range(g, g + GROUP)], axis=1
            )
            a = jnp.dot(d1[...], x, preferred_element_type=F32)
            turned = []
            for c in range(GROUP):
                re = a[:blocks, c * LANES:(c + 1) * LANES]
                im = a[blocks:, c * LANES:(c + 1) * LANES]
                turned.append(
                    jnp.concatenate(
                        [
                            (re * tw_at(0) + im * tw_at(1)).astype(BF16),
                            (im * tw_at(0) - re * tw_at(1)).astype(BF16),
                        ],
                        axis=1,
                    )
                )
            spec[g * blocks:(g + GROUP) * blocks, :] = jnp.dot(
                jnp.concatenate(turned, axis=0), fwd[...], preferred_element_type=F32
            )

    def inverse(left, right, sign, dst):
        for g in range(0, ch, GROUP):
            part = slice(g * blocks, (g + GROUP) * blocks)
            lr, li = left[part, :LANES], left[part, LANES:]
            rr, ri = right[part, :LANES], right[part, LANES:]
            if sign > 0:
                pr, pi = lr * rr - li * ri, lr * ri + li * rr
            else:
                pr, pi = lr * rr + li * ri, li * rr - lr * ri
            prod = jnp.concatenate([pr.astype(BF16), pi.astype(BF16)], axis=1)
            b = jnp.dot(prod, inv[...], preferred_element_type=F32)
            turned = []
            for c in range(GROUP):
                re = b[c * blocks:(c + 1) * blocks, :LANES]
                im = b[c * blocks:(c + 1) * blocks, LANES:]
                turned.append(
                    jnp.concatenate(
                        [
                            (re * tw_at(2) - im * tw_at(3)).astype(BF16),
                            (im * tw_at(2) + re * tw_at(3)).astype(BF16),
                        ],
                        axis=0,
                    )
                )
            y = jnp.dot(d4[...], jnp.concatenate(turned, axis=1), preferred_element_type=F32)
            for c in range(GROUP):
                y32[pl.ds(g + c, blocks, stride=ch), :] = y[:, c * LANES:(c + 1) * LANES]
        dst[...] = y32[...].astype(BF16)

    straight = rows(r_h, d * rows_half, rows_half)
    wait_bytes(straight, recv_sem.at[H])
    filter_pass = pair_copy(straight, straight, HP)
    filter_pass.start()
    wait_bytes(r_v, recv_sem.at[V])
    forward(r_v, spec_v)
    filter_pass.wait()
    forward(r_h, spec_h)
    inverse(spec_v, spec_h, 1, s_c)
    send_out(s_c, r_c, CO)

    wait_bytes(r_g, recv_sem.at[G])
    forward(r_g, spec_g)
    inverse(spec_g, spec_v, -1, s_gf)
    mine = rows(s_gf, d * rows_half, rows_half)
    grad_pass = pair_copy(rows(s_gf, (1 - d) * rows_half, rows_half), r_pair, GP)
    grad_pass.start()
    inverse(spec_g, spec_h, -1, s_gv)
    send_out(s_gv, r_gv, GV)
    grad_pass.wait()
    at = pl.ds(pl.multiple_of(d * rows_half, 16), rows_half)
    s_gf[at, :] = (s_gf[at, :].astype(F32) + r_pair[...].astype(F32)).astype(BF16)

    def send_grad(k, carry):
        slot = d * half + (my_slot + k) % half
        to = ((my_slot + k) % half) * 2 + d

        @pl.when(to != q)
        def _():
            pltpu.make_async_remote_copy(
                src_ref=rows(s_gf, slot * ch, ch), dst_ref=rows(r_gf, q * ch, ch),
                send_sem=send_sem.at[GF], recv_sem=recv_sem.at[GF],
                device_id={"ctx": to}, device_id_type=MESH,
            ).start()

        return carry

    lax.fori_loop(0, half, send_grad, 0)

    @pl.when(core == d)
    def _():
        pltpu.make_async_copy(rows(s_gf, my_slot * ch, ch), rows(r_gf, q * ch, ch), recv_sem.at[GF]).start()

    wait_bytes(r_c, recv_sem.at[CO])
    for j in range(chans // LANES):
        s = slice(j * LANES, (j + 1) * LANES)
        o_gg[:, s] = (in_gy[:, s].astype(F32) * r_c[s, :].astype(F32).T).astype(BF16)
    out_gg = pltpu.make_async_copy(o_gg, gg_hbm.at[0], out_sem.at[0])
    out_gg.start()

    wait_bytes(r_gv, recv_sem.at[GV])
    for j in range(chans // LANES):
        s = slice(j * LANES, (j + 1) * LANES)
        o_gv[:, s] = r_gv[s, :].astype(F32).T.astype(BF16)
    out_gv = pltpu.make_async_copy(o_gv, gv_hbm.at[0], out_sem.at[1])
    out_gv.start()

    wait_bytes(r_gf, recv_sem.at[GF])

    @pl.when(core == d)
    def _():
        last = pair_copy(r_gf, r_gf, GF)
        last.start()

    for j in range(chans // LANES):
        s = slice(j * LANES, (j + 1) * LANES)
        o_gf[:, s] = r_gf[s, :].astype(F32).T
    out_gf = pltpu.make_async_copy(o_gf, gf_hbm, out_sem.at[2])
    out_gf.start()

    most = (blocks - 1) * ch

    @pl.when(core == d)
    def _():
        wait_bytes(s_h.at[pl.ds(0, most), :], send_sem.at[H])
        wait_bytes(s_gf.at[pl.ds(0, rows_half - ch), :], send_sem.at[GF])
        wait_bytes(r_gf, send_sem.at[GF])

    @pl.when(core != d)
    def _():
        wait_bytes(s_gf.at[pl.ds(0, rows_half), :], send_sem.at[GF])

    for ref, sem in ((s_v, V), (s_g, G), (s_c, CO), (s_gv, GV)):
        wait_bytes(ref.at[pl.ds(0, most), :], send_sem.at[sem])
    out_gg.wait()
    out_gv.wait()
    out_gf.wait()


def body(values, gate_input, filter_param, grad_y, *tables):
    blocks = lax.axis_size("ctx")
    width, chans = filter_param.shape
    vm = lambda shape, kind: pltpu.VMEM(shape, kind)
    block = (width, chans)
    tiles = (chans, width)
    spec = (chans, 2 * width)
    any_spec = pl.BlockSpec(memory_space=pl.ANY)
    return pl.pallas_call(
        functools.partial(kernel, blocks),
        out_shape=(
            jax.ShapeDtypeStruct((1, width, chans), BF16),
            jax.ShapeDtypeStruct((1, width, chans), BF16),
            jax.ShapeDtypeStruct((width, chans), F32),
        ),
        in_specs=[any_spec] * 9,
        out_specs=(any_spec,) * 3,
        scratch_shapes=[vm(block, BF16)] * 4
        + [vm(t.shape, t.dtype) for t in tables]
        + [vm(tiles, BF16)] * 6
        + [vm(tiles, F32)] * 2
        + [vm(spec, F32)] * 3
        + [vm(tiles, BF16)] * 3
        + [vm((chans // 2, width), BF16)]
        + [vm(tiles, BF16)] * 3
        + [vm(block, BF16)] * 2
        + [vm(block, F32)]
        + [
            pltpu.SemaphoreType.DMA((9,)),
            pltpu.SemaphoreType.DMA((9,)),
            pltpu.SemaphoreType.DMA((9,)),
            pltpu.SemaphoreType.DMA((3,)),
        ],
        compiler_params=pltpu.CompilerParams(
            collective_id=0, has_side_effects=True, vmem_limit_bytes=40 * 1024 * 1024
        ),
        cost_estimate=pl.CostEstimate(flops=1_000_000_000, bytes_accessed=4_000_000, transcendentals=0),
    )(values, gate_input, filter_param, grad_y, *tables)


def solution(mesh):
    blocks = mesh.shape["ctx"]
    tables = make_tables(blocks, LANES)
    placed = (P("dp", "ctx", "tp"), P("dp", "ctx", "tp"), P("ctx", "tp"), P("dp", "ctx", "tp"))
    mapped = jax.shard_map(
        body,
        mesh=mesh,
        in_specs=placed + (P(),) * len(tables),
        out_specs=(P("dp", "ctx", "tp"), P("dp", "ctx", "tp"), P("ctx", "tp")),
        check_vma=False,
    )

    def run(values, gate_input, filter_param, grad_y):
        return mapped(values, gate_input, filter_param, grad_y, *tables)

    return run
```

time: 869 us -> 102 us (0.12)
  the two profiles are of different devices: /device:TPU:1 before, /device:TPU:46 now
where the time goes in v1:
time: 102 us
  Pallas kernels  91 us (89%)
  local copies, waits for them, and re-layouts  10.2 us (10%)
    pallas_call x1, Pallas kernels, body(): pl.pallas_call(functools.partial(kernel, blocks), out_shape=(jax.ShapeDty...  91 us
    unnamed x21, local copies, waits for them, and re-layouts  10.2 us

profile of v1, /device:TPU:46, one launch (start us, length us, event | category | flops | bytes accessed | tf_op | source)
XLA Modules:
  0.0 101.9 jit_solution(4392097430434782596)
XLA Ops:
  0.6 0.0 copy-start
  0.6 0.9 copy-done
  1.6 0.0 copy-start.1
  1.6 0.9 copy-done.1
  2.5 0.0 copy-start.2
  2.5 0.9 copy-done.2
  3.5 0.0 copy-start.3
  3.5 0.9 copy-done.3
  4.4 0.0 copy-start.4
  4.4 0.9 copy-done.4
  5.3 0.0 copy-start.5
  5.3 0.9 copy-done.5
  6.2 0.0 copy-start.6
  6.2 0.9 copy-done.6
  7.1 0.0 copy-start.7
  7.2 0.8 copy-done.7
  7.9 0.0 copy-start.8
  7.9 0.7 copy-done.8
  8.6 91.0 %shard_map.112 = (bf16[1,128,1024]{2,1,0:T(8,128)(2,1)S(1)}, bf16[1,128,1024]{2,1,0:T(8,128)(2,1)S(1)}, f32[128,1024]{1,0:T(8,128)S(1)}) custom-call(bf16[1,128,1024]{2,1,0:T(8,128)(2,1)S(1)} %copy-done, bf16[1,128,1024]{2,1,0:T(8,128)(2,1)S(1)} %copy-done.1, bf16[128,1024]{1,0:T(8,128)(2,1)S(1)} %copy-done.2, bf16[1,128,1024]{2,1,0:T(8,128)(2,1)S(1)} %copy-done.3, ...), custom_call_target="tpu_custom_call" | custom-call | flops 1000000000 | bytes 4000000 | tf_op jit(solution)/shard_map/pallas_call | solution.py:312
  99.7 0.7 copy.15
  100.4 0.7 copy.16
  101.1 0.8 copy.17
Async XLA Ops:
  0.6 1.0 copy-start
  1.6 0.9 copy-start.1
  2.5 0.9 copy-start.2
  3.5 0.9 copy-start.3
  4.4 0.9 copy-start.4
  5.3 0.9 copy-start.5
  6.2 0.9 copy-start.6
  7.1 0.8 copy-start.7
  7.9 0.7 copy-start.8

commit v2 on v1

--- a/solution.py
+++ b/solution.py
@@ -78,8 +78,9 @@
 
     def peer(k):
         step, e = k // 4, k % 4
-        dist = (step + 1) // 2
-        dz = jnp.where(step % 2 == 1, dist, zs - dist)
+        turn = step // 2
+        dist = (turn + 1) // 2
+        dz = jnp.where(turn % 2 == 1, zs - dist, dist) + (step % 2) * (zs // 2)
         return ((my_z + dz) % zs) * 4 + (my_e + e) % 4
 
     barrier = pltpu.get_barrier_semaphore()
@@ -115,8 +116,9 @@
 
         lax.fori_loop(1, blocks, one, 0)
 
-    def send_out(src, dst, sem):
-        pltpu.make_async_copy(rows(src, my_slot * ch, ch), rows(dst, q * ch, ch), recv_sem.at[sem]).start()
+    def send_out(src, dst, sem, first=0, last=blocks):
+        if first == 0:
+            pltpu.make_async_copy(rows(src, my_slot * ch, ch), rows(dst, q * ch, ch), recv_sem.at[sem]).start()
 
         def one(k, carry):
             to = peer(k)
@@ -128,7 +130,7 @@
             ).start()
             return carry
 
-        lax.fori_loop(1, blocks, one, 0)
+        lax.fori_loop(max(first, 1), last, one, 0)
 
     def pair_copy(src, dst, sem):
         return pltpu.make_async_remote_copy(
@@ -152,7 +154,6 @@
     loads[2].wait()
     loads[3].wait()
     transpose_in(lambda s: (in_gy[:, s].astype(F32) * in_gate[:, s].astype(F32)).astype(BF16).astype(F32), s_g)
-    send_in(s_g, r_g, G)
     for load in loads[4:]:
         load.wait()
 
@@ -216,6 +217,7 @@
     wait_bytes(straight, recv_sem.at[H])
     filter_pass = pair_copy(straight, straight, HP)
     filter_pass.start()
+    send_in(s_g, r_g, G)
     wait_bytes(r_v, recv_sem.at[V])
     forward(r_v, spec_v)
     filter_pass.wait()
@@ -230,14 +232,14 @@
     grad_pass = pair_copy(rows(s_gf, (1 - d) * rows_half, rows_half), r_pair, GP)
     grad_pass.start()
     inverse(spec_g, spec_h, -1, s_gv)
-    send_out(s_gv, r_gv, GV)
+    send_out(s_gv, r_gv, GV, 0, half)
     grad_pass.wait()
     at = pl.ds(pl.multiple_of(d * rows_half, 16), rows_half)
     s_gf[at, :] = (s_gf[at, :].astype(F32) + r_pair[...].astype(F32)).astype(BF16)
 
     def send_grad(k, carry):
-        slot = d * half + (my_slot + k) % half
-        to = ((my_slot + k) % half) * 2 + d
+        to = peer((k // 2) * 4 + (k % 2) * 2 + (core + d) % 2)
+        slot = d * half + to // 2
 
         @pl.when(to != q)
         def _():
@@ -255,6 +257,8 @@
     def _():
         pltpu.make_async_copy(rows(s_gf, my_slot * ch, ch), rows(r_gf, q * ch, ch), recv_sem.at[GF]).start()
 
+    send_out(s_gv, r_gv, GV, half, blocks)
+
     wait_bytes(r_c, recv_sem.at[CO])
     for j in range(chans // LANES):
         s = slice(j * LANES, (j + 1) * LANES)
@@ -262,6 +266,20 @@
     out_gg = pltpu.make_async_copy(o_gg, gg_hbm.at[0], out_sem.at[0])
     out_gg.start()
 
+    out_gf = pltpu.make_async_copy(o_gf, gf_hbm, out_sem.at[2])
+
+    def give_gf():
+        for j in range(chans // LANES):
+            s = slice(j * LANES, (j + 1) * LANES)
+            o_gf[:, s] = r_gf[s, :].astype(F32).T
+        out_gf.start()
+
+    @pl.when(core == d)
+    def _():
+        wait_bytes(r_gf, recv_sem.at[GF])
+        pair_copy(r_gf, r_gf, GF).start()
+        give_gf()
+
     wait_bytes(r_gv, recv_sem.at[GV])
     for j in range(chans // LANES):
         s = slice(j * LANES, (j + 1) * LANES)
@@ -269,18 +287,10 @@
     out_gv = pltpu.make_async_copy(o_gv, gv_hbm.at[0], out_sem.at[1])
     out_gv.start()
 
-    wait_bytes(r_gf, recv_sem.at[GF])
-
-    @pl.when(core == d)
-    def _():
-        last = pair_copy(r_gf, r_gf, GF)
-        last.start()
-
-    for j in range(chans // LANES):
-        s = slice(j * LANES, (j + 1) * LANES)
-        o_gf[:, s] = r_gf[s, :].astype(F32).T
-    out_gf = pltpu.make_async_copy(o_gf, gf_hbm, out_sem.at[2])
-    out_gf.start()
+    @pl.when(core != d)
+    def _():
+        wait_bytes(r_gf, recv_sem.at[GF])
+        give_gf()
 
     most = (blocks - 1) * ch
 
@@ -335,7 +345,7 @@
             pltpu.SemaphoreType.DMA((3,)),
         ],
         compiler_params=pltpu.CompilerParams(
-            collective_id=0, has_side_effects=True, vmem_limit_bytes=40 * 1024 * 1024
+            collective_id=0, has_side_effects=True, vmem_limit_bytes=64 * 1024 * 1024
         ),
         cost_estimate=pl.CostEstimate(flops=1_000_000_000, bytes_accessed=4_000_000, transcendentals=0),
     )(values, gate_input, filter_param, grad_y, *tables)

time: 102 us -> 84.9 us (0.83)
  the two profiles are of different devices: /device:TPU:46 before, /device:TPU:1 now
where the time goes in v2:
time: 84.9 us; the launch traced here: 84.7 us
  Pallas kernels  80.8 us (95%)
  local copies, waits for them, and re-layouts  3.24 us (4%)
    pallas_call x1, Pallas kernels, body(): pl.pallas_call(functools.partial(kernel, blocks), out_shape=(jax.ShapeDty...  80.8 us
    unnamed x7, local copies, waits for them, and re-layouts  3.24 us

profile of v2, /device:TPU:1, one launch (start us, length us, event | category | flops | bytes accessed | tf_op | source)
XLA Modules:
  0.0 84.7 jit_solution(15945103522613091590)
XLA Ops:
  0.6 80.8 %shard_map.112 = (bf16[1,128,1024]{2,1,0:T(8,128)(2,1)}, bf16[1,128,1024]{2,1,0:T(8,128)(2,1)}, f32[128,1024]{1,0:T(8,128)}) custom-call(bf16[1,128,1024]{2,1,0:T(8,128)(2,1)} %v_hbm.1, bf16[1,128,1024]{2,1,0:T(8,128)(2,1)} %gate_hbm.1, bf16[128,1024]{1,0:T(8,128)(2,1)} %f_hbm.1, bf16[1,128,1024]{2,1,0:T(8,128)(2,1)} %gy_hbm.1, ...), custom_call_target="tpu_custom_call" | custom-call | flops 1000000000 | bytes 4000000 | tf_op jit(solution)/shard_map/pallas_call | solution.py:322
  81.4 0.0 copy-start.1
  81.5 0.0 copy-start
  81.5 1.7 %copy.15 = bf16[1,128,1024]{2,1,0:T(8,128)(2,1)} copy(bf16[1,128,1024]{2,1,0:T(8,128)(2,1)} %get-tuple-element.6) | data formatting | bytes 524288
  83.2 0.0 copy-done.1
  83.2 0.7 copy.16
  83.9 0.0 copy-done
  83.9 0.8 copy.17
Async XLA Ops:
  81.4 1.8 %copy-start.1 = (bf16[1,128,1024]{2,1,0:T(8,128)(2,1)S(1)}, bf16[1,128,1024]{2,1,0:T(8,128)(2,1)}, u32[]{:S(2)}) copy-start(bf16[1,128,1024]{2,1,0:T(8,128)(2,1)} %get-tuple-element.7) | copy-start | bytes 786436
  81.5 2.5 %copy-start = (f32[128,1024]{1,0:T(8,128)S(1)}, f32[128,1024]{1,0:T(8,128)}, u32[]{:S(2)}) copy-start(f32[128,1024]{1,0:T(8,128)} %get-tuple-element.8) | copy-start | bytes 1572868

commit v3 on v2

--- a/solution.py
+++ b/solution.py
@@ -311,6 +311,16 @@
     out_gf.wait()
 
 
+def copy_kernel(*refs):
+    count = len(refs) // 2
+    sems = refs[-1]
+    copies = [pltpu.make_async_copy(refs[i], refs[count + i], sems.at[i]) for i in range(count)]
+    for copy in copies:
+        copy.start()
+    for copy in copies:
+        copy.wait()
+
+
 def body(values, gate_input, filter_param, grad_y, *tables):
     blocks = lax.axis_size("ctx")
     width, chans = filter_param.shape
@@ -319,13 +329,15 @@
     tiles = (chans, width)
     spec = (chans, 2 * width)
     any_spec = pl.BlockSpec(memory_space=pl.ANY)
-    return pl.pallas_call(
+    out_shape = (
+        jax.ShapeDtypeStruct((1, width, chans), BF16),
+        jax.ShapeDtypeStruct((1, width, chans), BF16),
+        jax.ShapeDtypeStruct((width, chans), F32),
+    )
+    operands = [pltpu.with_memory_space_constraint(x, pltpu.HBM) for x in (values, gate_input, filter_param, grad_y, *tables)]
+    results = pl.pallas_call(
         functools.partial(kernel, blocks),
-        out_shape=(
-            jax.ShapeDtypeStruct((1, width, chans), BF16),
-            jax.ShapeDtypeStruct((1, width, chans), BF16),
-            jax.ShapeDtypeStruct((width, chans), F32),
-        ),
+        out_shape=out_shape,
         in_specs=[any_spec] * 9,
         out_specs=(any_spec,) * 3,
         scratch_shapes=[vm(block, BF16)] * 4
@@ -345,10 +357,18 @@
             pltpu.SemaphoreType.DMA((3,)),
         ],
         compiler_params=pltpu.CompilerParams(
-            collective_id=0, has_side_effects=True, vmem_limit_bytes=64 * 1024 * 1024
+            collective_id=0, has_side_effects=True, vmem_limit_bytes=40 * 1024 * 1024
         ),
         cost_estimate=pl.CostEstimate(flops=1_000_000_000, bytes_accessed=4_000_000, transcendentals=0),
-    )(values, gate_input, filter_param, grad_y, *tables)
+    )(*operands)
+    return pl.pallas_call(
+        copy_kernel,
+        out_shape=out_shape,
+        in_specs=[any_spec] * 3,
+        out_specs=(any_spec,) * 3,
+        scratch_shapes=[pltpu.SemaphoreType.DMA((3,))],
+        compiler_params=pltpu.CompilerParams(vmem_limit_bytes=4 * 1024 * 1024),
+    )(*results)
 
 
 def solution(mesh):

time: 84.9 us -> 81.9 us (0.965)
  local copies, waits for them, and re-layouts: 3.24 us -> 0 us
    unnamed x7 -> x0, local copies, waits for them, and re-layouts: 3.24 us -> none
    pallas_call x1 -> x2, Pallas kernels: 80.8 us -> 81.1 us  [the longest x1 80.1 us: body(): pl.pallas_call(functools.partial(kernel, blocks), out_shape=out_shape, in...]
where the time goes in v3:
time: 81.9 us; the launch traced here: 81.7 us
  Pallas kernels  81.1 us (99%)
    pallas_call x1, Pallas kernels, body(): pl.pallas_call(functools.partial(kernel, blocks), out_shape=out_shape, in...  80.1 us

profile of v3, /device:TPU:1, one launch (start us, length us, event | category | flops | bytes accessed | tf_op | source)
XLA Modules:
  0.0 81.7 jit_solution(4358112007880540284)
XLA Ops:
  0.6 80.1 %shard_map.112 = (bf16[1,128,1024]{2,1,0:T(8,128)(2,1)S(1)}, bf16[1,128,1024]{2,1,0:T(8,128)(2,1)S(1)}, f32[128,1024]{1,0:T(8,128)S(1)}) custom-call(bf16[1,128,1024]{2,1,0:T(8,128)(2,1)} %v_hbm.1, bf16[1,128,1024]{2,1,0:T(8,128)(2,1)} %gate_hbm.1, bf16[128,1024]{1,0:T(8,128)(2,1)} %f_hbm.1, bf16[1,128,1024]{2,1,0:T(8,128)(2,1)} %gy_hbm.1, ...), custom_call_target="tpu_custom_call" | custom-call | flops 1000000000 | bytes 4000000 | tf_op jit(solution)/shard_map/pallas_call | solution.py:338
  80.7 1.0 %shard_map.113 = (bf16[1,128,1024]{2,1,0:T(8,128)(2,1)}, bf16[1,128,1024]{2,1,0:T(8,128)(2,1)}, f32[128,1024]{1,0:T(8,128)}) custom-call(bf16[1,128,1024]{2,1,0:T(8,128)(2,1)S(1)} %get-tuple-element.6.refs_0_, bf16[1,128,1024]{2,1,0:T(8,128)(2,1)S(1)} %get-tuple-element.7.refs_1_, f32[128,1024]{1,0:T(8,128)S(1)} %get-tuple-element.8.refs_2_), custom_call_target="tpu_custom_call" | custom-call | tf_op jit(solution)/shard_map/pallas_call | solution.py:364

commit v4 on v3

--- a/solution.py
+++ b/solution.py
@@ -73,24 +73,22 @@
             ]
         )
     ]
-    for load in loads:
-        load.start()
-
-    def peer(k):
+    loads[0].start()
+
+    def peer(k, turned=0):
         step, e = k // 4, k % 4
         turn = step // 2
         dist = (turn + 1) // 2
-        dz = jnp.where(turn % 2 == 1, zs - dist, dist) + (step % 2) * (zs // 2)
-        return ((my_z + dz) % zs) * 4 + (my_e + e) % 4
+        dz = (zs - dist if turn % 2 else dist) + step % 2 * (zs // 2)
+        return lax.rem(my_z + dz, zs) * 4 + lax.rem(my_e + e + turned, 4)
 
     barrier = pltpu.get_barrier_semaphore()
 
-    def greet(k, carry):
+    for k in range(1, blocks):
         pl.semaphore_signal(barrier, inc=1, device_id={"ctx": peer(k)}, device_id_type=MESH)
-        return carry
-
-    lax.fori_loop(1, blocks, greet, 0)
     pl.semaphore_signal(barrier, inc=1, device_id={"dp": 1 - d}, device_id_type=MESH)
+    for load in loads[1:]:
+        load.start()
 
     def rows(ref, start, count):
         return ref.at[pl.ds(pl.multiple_of(start, 16), count), :]
@@ -105,32 +103,26 @@
     def send_in(src, dst, sem):
         pltpu.make_async_copy(rows(src, q * ch, ch), rows(dst, my_slot * ch, ch), recv_sem.at[sem]).start()
 
-        def one(k, carry):
+        for k in range(1, blocks):
             to = peer(k)
             pltpu.make_async_remote_copy(
                 src_ref=rows(src, to * ch, ch), dst_ref=rows(dst, my_slot * ch, ch),
                 send_sem=send_sem.at[sem], recv_sem=recv_sem.at[sem],
                 device_id={"ctx": to}, device_id_type=MESH,
             ).start()
-            return carry
-
-        lax.fori_loop(1, blocks, one, 0)
 
     def send_out(src, dst, sem, first=0, last=blocks):
         if first == 0:
             pltpu.make_async_copy(rows(src, my_slot * ch, ch), rows(dst, q * ch, ch), recv_sem.at[sem]).start()
 
-        def one(k, carry):
+        for k in range(max(first, 1), last):
             to = peer(k)
-            slot = (to % 2) * half + to // 2
+            slot = lax.rem(to, 2) * half + lax.div(to, 2)
             pltpu.make_async_remote_copy(
                 src_ref=rows(src, slot * ch, ch), dst_ref=rows(dst, q * ch, ch),
                 send_sem=send_sem.at[sem], recv_sem=recv_sem.at[sem],
                 device_id={"ctx": to}, device_id_type=MESH,
             ).start()
-            return carry
-
-        lax.fori_loop(max(first, 1), last, one, 0)
 
     def pair_copy(src, dst, sem):
         return pltpu.make_async_remote_copy(
@@ -141,7 +133,11 @@
     H, V, G, HP, CO, GV, GP, GF, GFP = range(9)
 
     loads[0].wait()
-    transpose_in(lambda s: in_f[:, s].astype(F32), s_h)
+
+    @pl.when(core == d)
+    def _():
+        transpose_in(lambda s: in_f[:, s].astype(F32), s_h)
+
     pl.semaphore_wait(barrier, blocks)
 
     @pl.when(core == d)
@@ -237,25 +233,26 @@
     at = pl.ds(pl.multiple_of(d * rows_half, 16), rows_half)
     s_gf[at, :] = (s_gf[at, :].astype(F32) + r_pair[...].astype(F32)).astype(BF16)
 
-    def send_grad(k, carry):
-        to = peer((k // 2) * 4 + (k % 2) * 2 + (core + d) % 2)
-        slot = d * half + to // 2
-
-        @pl.when(to != q)
-        def _():
-            pltpu.make_async_remote_copy(
-                src_ref=rows(s_gf, slot * ch, ch), dst_ref=rows(r_gf, q * ch, ch),
-                send_sem=send_sem.at[GF], recv_sem=recv_sem.at[GF],
-                device_id={"ctx": to}, device_id_type=MESH,
-            ).start()
-
-        return carry
-
-    lax.fori_loop(0, half, send_grad, 0)
+    odd = lax.rem(core + d, 2)
+
+    def send_grad(k):
+        to = peer(k, odd)
+        pltpu.make_async_remote_copy(
+            src_ref=rows(s_gf, (d * half + lax.div(to, 2)) * ch, ch), dst_ref=rows(r_gf, q * ch, ch),
+            send_sem=send_sem.at[GF], recv_sem=recv_sem.at[GF],
+            device_id={"ctx": to}, device_id_type=MESH,
+        ).start()
+
+    for k in range(2, blocks, 2):
+        send_grad(k)
 
     @pl.when(core == d)
     def _():
         pltpu.make_async_copy(rows(s_gf, my_slot * ch, ch), rows(r_gf, q * ch, ch), recv_sem.at[GF]).start()
+
+    @pl.when(core != d)
+    def _():
+        send_grad(0)
 
     send_out(s_gv, r_gv, GV, half, blocks)
 

time: 81.9 us -> 80.9 us (0.988)
  Pallas kernels: 81.1 us -> 80.1 us
    pallas_call x1, Pallas kernels: 80.1 us -> 79.1 us  [body(): pl.pallas_call(functools.partial(kernel, blocks), out_shape=out_shape, in...]
where the time goes in v4:
time: 80.9 us; the launch traced here: 80.7 us
  Pallas kernels  80.1 us (99%)
    pallas_call x1, Pallas kernels, body(): pl.pallas_call(functools.partial(kernel, blocks), out_shape=out_shape, in...  79.1 us

profile of v4, /device:TPU:1, one launch (start us, length us, event | category | flops | bytes accessed | tf_op | source)
XLA Modules:
  0.0 80.7 jit_solution(5620292264667872839)
XLA Ops:
  0.6 79.1 %shard_map.112 = (bf16[1,128,1024]{2,1,0:T(8,128)(2,1)S(1)}, bf16[1,128,1024]{2,1,0:T(8,128)(2,1)S(1)}, f32[128,1024]{1,0:T(8,128)S(1)}) custom-call(bf16[1,128,1024]{2,1,0:T(8,128)(2,1)} %v_hbm.1, bf16[1,128,1024]{2,1,0:T(8,128)(2,1)} %gate_hbm.1, bf16[128,1024]{1,0:T(8,128)(2,1)} %f_hbm.1, bf16[1,128,1024]{2,1,0:T(8,128)(2,1)} %gy_hbm.1, ...), custom_call_target="tpu_custom_call" | custom-call | flops 1000000000 | bytes 4000000 | tf_op jit(solution)/shard_map/pallas_call | solution.py:335
  79.7 1.0 %shard_map.113 = (bf16[1,128,1024]{2,1,0:T(8,128)(2,1)}, bf16[1,128,1024]{2,1,0:T(8,128)(2,1)}, f32[128,1024]{1,0:T(8,128)}) custom-call(bf16[1,128,1024]{2,1,0:T(8,128)(2,1)S(1)} %get-tuple-element.6.refs_0_, bf16[1,128,1024]{2,1,0:T(8,128)(2,1)S(1)} %get-tuple-element.7.refs_1_, f32[128,1024]{1,0:T(8,128)S(1)} %get-tuple-element.8.refs_2_), custom_call_target="tpu_custom_call" | custom-call | tf_op jit(solution)/shard_map/pallas_call | solution.py:361

commit v5 on v4

--- a/solution.py
+++ b/solution.py
@@ -3,6 +3,7 @@
 
 import jax
 import jax.numpy as jnp
+import ml_dtypes
 import numpy as np
 from jax import lax
 from jax.experimental import pallas as pl
@@ -32,9 +33,15 @@
     co, si = np.cos(ang3), np.sin(ang3)
     fwd = np.block([[co, -si], [si, co]])
     inv = np.block([[co, si], [-si, co]])
+
+    def two_parts(table, axis):
+        high = np.asarray(table, ml_dtypes.bfloat16)
+        low = np.asarray(table - high.astype(np.float64), ml_dtypes.bfloat16)
+        return jnp.asarray(np.concatenate([high, low], axis=axis))
+
     return (
-        jnp.asarray(d1, BF16),
-        jnp.asarray(d4, BF16),
+        two_parts(d1, 1),
+        two_parts(d4, 1),
         jnp.asarray(np.concatenate([tw, tw * scale], axis=1), F32),
         jnp.asarray(fwd, BF16),
         jnp.asarray(inv, BF16),
@@ -156,13 +163,16 @@
     def tw_at(i):
         return tw[:, i * LANES:(i + 1) * LANES]
 
+    def two_dots(left, table):
+        return jnp.dot(left, table[...], preferred_element_type=F32)
+
     def forward(src, spec):
         x32[...] = src[...].astype(F32)
         for g in range(0, ch, GROUP):
             x = jnp.concatenate(
                 [x32[pl.ds(c, blocks, stride=ch), :].astype(BF16) for c in range(g, g + GROUP)], axis=1
             )
-            a = jnp.dot(d1[...], x, preferred_element_type=F32)
+            a = jnp.dot(d1[...], jnp.concatenate([x, x], axis=0), preferred_element_type=F32)
             turned = []
             for c in range(GROUP):
                 re = a[:blocks, c * LANES:(c + 1) * LANES]
@@ -176,9 +186,7 @@
                         axis=1,
                     )
                 )
-            spec[g * blocks:(g + GROUP) * blocks, :] = jnp.dot(
-                jnp.concatenate(turned, axis=0), fwd[...], preferred_element_type=F32
-            )
+            spec[g * blocks:(g + GROUP) * blocks, :] = two_dots(jnp.concatenate(turned, axis=0), fwd)
 
     def inverse(left, right, sign, dst):
         for g in range(0, ch, GROUP):
@@ -190,7 +198,7 @@
             else:
                 pr, pi = lr * rr + li * ri, li * rr - lr * ri
             prod = jnp.concatenate([pr.astype(BF16), pi.astype(BF16)], axis=1)
-            b = jnp.dot(prod, inv[...], preferred_element_type=F32)
+            b = two_dots(prod, inv)
             turned = []
             for c in range(GROUP):
                 re = b[c * blocks:(c + 1) * blocks, :LANES]
@@ -204,7 +212,8 @@
                         axis=0,
                     )
                 )
-            y = jnp.dot(d4[...], jnp.concatenate(turned, axis=1), preferred_element_type=F32)
+            both = jnp.concatenate(turned, axis=1)
+            y = jnp.dot(d4[...], jnp.concatenate([both, both], axis=0), preferred_element_type=F32)
             for c in range(GROUP):
                 y32[pl.ds(g + c, blocks, stride=ch), :] = y[:, c * LANES:(c + 1) * LANES]
         dst[...] = y32[...].astype(BF16)

time: 80.9 us -> 80.7 us (level)
  no operation moved by 1% of the time
where the time goes in v5:
time: 80.7 us; the launch traced here: 80.6 us
  Pallas kernels  79.9 us (99%)
    pallas_call x1, Pallas kernels, body(): pl.pallas_call(functools.partial(kernel, blocks), out_shape=out_shape, in...  78.9 us

profile of v5, /device:TPU:1, one launch (start us, length us, event | category | flops | bytes accessed | tf_op | source)
XLA Modules:
  0.0 80.6 jit_solution(12593855249767238686)
XLA Ops:
  0.6 78.9 %shard_map.112 = (bf16[1,128,1024]{2,1,0:T(8,128)(2,1)S(1)}, bf16[1,128,1024]{2,1,0:T(8,128)(2,1)S(1)}, f32[128,1024]{1,0:T(8,128)S(1)}) custom-call(bf16[1,128,1024]{2,1,0:T(8,128)(2,1)} %v_hbm.1, bf16[1,128,1024]{2,1,0:T(8,128)(2,1)} %gate_hbm.1, bf16[128,1024]{1,0:T(8,128)(2,1)} %f_hbm.1, bf16[1,128,1024]{2,1,0:T(8,128)(2,1)} %gy_hbm.1, ...), custom_call_target="tpu_custom_call" | custom-call | flops 1000000000 | bytes 4000000 | tf_op jit(solution)/shard_map/pallas_call | solution.py:344
  79.6 1.0 %shard_map.113 = (bf16[1,128,1024]{2,1,0:T(8,128)(2,1)}, bf16[1,128,1024]{2,1,0:T(8,128)(2,1)}, f32[128,1024]{1,0:T(8,128)}) custom-call(bf16[1,128,1024]{2,1,0:T(8,128)(2,1)S(1)} %get-tuple-element.6.refs_0_, bf16[1,128,1024]{2,1,0:T(8,128)(2,1)S(1)} %get-tuple-element.7.refs_1_, f32[128,1024]{1,0:T(8,128)S(1)} %get-tuple-element.8.refs_2_), custom_call_target="tpu_custom_call" | custom-call | tf_op jit(solution)/shard_map/pallas_call | solution.py:370

commit v6 on v5

--- a/solution.py
+++ b/solution.py
@@ -51,13 +51,12 @@
 def kernel(
     blocks,
     v_hbm, gate_hbm, f_hbm, gy_hbm, d1_hbm, d4_hbm, tw_hbm, fwd_hbm, inv_hbm,
-    gg_hbm, gv_hbm, gf_hbm,
+    o_gg, o_gv, o_gf,
     in_v, in_gate, in_f, in_gy, d1, d4, tw, fwd, inv,
     s_h, s_v, s_g, r_h, r_v, r_g,
     x32, y32, spec_h, spec_v, spec_g,
     s_c, s_gv, s_gf, r_pair, r_c, r_gv, r_gf,
-    o_gg, o_gv, o_gf,
-    in_sem, send_sem, recv_sem, out_sem,
+    in_sem, send_sem, recv_sem,
 ):
     chans = in_v.shape[1]
     width = in_v.shape[0]
@@ -268,17 +267,13 @@
     wait_bytes(r_c, recv_sem.at[CO])
     for j in range(chans // LANES):
         s = slice(j * LANES, (j + 1) * LANES)
-        o_gg[:, s] = (in_gy[:, s].astype(F32) * r_c[s, :].astype(F32).T).astype(BF16)
-    out_gg = pltpu.make_async_copy(o_gg, gg_hbm.at[0], out_sem.at[0])
-    out_gg.start()
-
-    out_gf = pltpu.make_async_copy(o_gf, gf_hbm, out_sem.at[2])
+        o_gg[0, :, s] = (in_gy[:, s].astype(F32) * r_c[s, :].astype(F32).T).astype(BF16)
+
 
     def give_gf():
         for j in range(chans // LANES):
             s = slice(j * LANES, (j + 1) * LANES)
             o_gf[:, s] = r_gf[s, :].astype(F32).T
-        out_gf.start()
 
     @pl.when(core == d)
     def _():
@@ -289,9 +284,7 @@
     wait_bytes(r_gv, recv_sem.at[GV])
     for j in range(chans // LANES):
         s = slice(j * LANES, (j + 1) * LANES)
-        o_gv[:, s] = r_gv[s, :].astype(F32).T.astype(BF16)
-    out_gv = pltpu.make_async_copy(o_gv, gv_hbm.at[0], out_sem.at[1])
-    out_gv.start()
+        o_gv[0, :, s] = r_gv[s, :].astype(F32).T.astype(BF16)
 
     @pl.when(core != d)
     def _():
@@ -312,9 +305,6 @@
 
     for ref, sem in ((s_v, V), (s_g, G), (s_c, CO), (s_gv, GV)):
         wait_bytes(ref.at[pl.ds(0, most), :], send_sem.at[sem])
-    out_gg.wait()
-    out_gv.wait()
-    out_gf.wait()
 
 
 def copy_kernel(*refs):
@@ -345,7 +335,7 @@
         functools.partial(kernel, blocks),
         out_shape=out_shape,
         in_specs=[any_spec] * 9,
-        out_specs=(any_spec,) * 3,
+        out_specs=(pl.BlockSpec(memory_space=pltpu.VMEM),) * 3,
         scratch_shapes=[vm(block, BF16)] * 4
         + [vm(t.shape, t.dtype) for t in tables]
         + [vm(tiles, BF16)] * 6
@@ -354,13 +344,10 @@
         + [vm(tiles, BF16)] * 3
         + [vm((chans // 2, width), BF16)]
         + [vm(tiles, BF16)] * 3
-        + [vm(block, BF16)] * 2
-        + [vm(block, F32)]
         + [
             pltpu.SemaphoreType.DMA((9,)),
             pltpu.SemaphoreType.DMA((9,)),
             pltpu.SemaphoreType.DMA((9,)),
-            pltpu.SemaphoreType.DMA((3,)),
         ],
         compiler_params=pltpu.CompilerParams(
             collective_id=0, has_side_effects=True, vmem_limit_bytes=40 * 1024 * 1024

time: 80.7 us -> 80.6 us (level)
  no operation moved by 1% of the time
where the time goes in v6:
time: 80.6 us; the launch traced here: 80.5 us
  Pallas kernels  79.8 us (99%)
    pallas_call x1, Pallas kernels, body(): pl.pallas_call(functools.partial(kernel, blocks), out_shape=out_shape, in...  78.8 us

profile of v6, /device:TPU:1, one launch (start us, length us, event | category | flops | bytes accessed | tf_op | source)
XLA Modules:
  0.0 80.5 jit_solution(15658961639879492688)
XLA Ops:
  0.6 78.8 %shard_map.112 = (bf16[1,128,1024]{2,1,0:T(8,128)(2,1)S(1)}, bf16[1,128,1024]{2,1,0:T(8,128)(2,1)S(1)}, f32[128,1024]{1,0:T(8,128)S(1)}) custom-call(bf16[1,128,1024]{2,1,0:T(8,128)(2,1)} %v_hbm.1, bf16[1,128,1024]{2,1,0:T(8,128)(2,1)} %gate_hbm.1, bf16[128,1024]{1,0:T(8,128)(2,1)} %f_hbm.1, bf16[1,128,1024]{2,1,0:T(8,128)(2,1)} %gy_hbm.1, ...), custom_call_target="tpu_custom_call" | custom-call | flops 1000000000 | bytes 4000000 | tf_op jit(solution)/shard_map/pallas_call | solution.py:334
  79.5 1.0 %shard_map.113 = (bf16[1,128,1024]{2,1,0:T(8,128)(2,1)}, bf16[1,128,1024]{2,1,0:T(8,128)(2,1)}, f32[128,1024]{1,0:T(8,128)}) custom-call(bf16[1,128,1024]{2,1,0:T(8,128)(2,1)S(1)} %get-tuple-element.6.refs_0_, bf16[1,128,1024]{2,1,0:T(8,128)(2,1)S(1)} %get-tuple-element.7.refs_1_, f32[128,1024]{1,0:T(8,128)S(1)} %get-tuple-element.8.refs_2_), custom_call_target="tpu_custom_call" | custom-call | tf_op jit(solution)/shard_map/pallas_call | solution.py:357

commit v7 on v6

--- a/solution.py
+++ b/solution.py
@@ -14,7 +14,7 @@
 F32 = jnp.float32
 BF16 = jnp.bfloat16
 LANES = 128
-GROUP = 4
+GROUP = 8
 
 
 def make_tables(blocks, width):

time: 80.6 us -> 80.7 us (level)
  no operation moved by 1% of the time
where the time goes in v7:
time: 80.7 us; the launch traced here: 80.5 us
  Pallas kernels  79.9 us (99%)
    pallas_call x1, Pallas kernels, body(): pl.pallas_call(functools.partial(kernel, blocks), out_shape=out_shape, in...  78.9 us

profile of v7, /device:TPU:1, one launch (start us, length us, event | category | flops | bytes accessed | tf_op | source)
XLA Modules:
  0.0 80.5 jit_solution(1999739286094239306)
XLA Ops:
  0.6 78.9 %shard_map.112 = (bf16[1,128,1024]{2,1,0:T(8,128)(2,1)S(1)}, bf16[1,128,1024]{2,1,0:T(8,128)(2,1)S(1)}, f32[128,1024]{1,0:T(8,128)S(1)}) custom-call(bf16[1,128,1024]{2,1,0:T(8,128)(2,1)} %v_hbm.1, bf16[1,128,1024]{2,1,0:T(8,128)(2,1)} %gate_hbm.1, bf16[128,1024]{1,0:T(8,128)(2,1)} %f_hbm.1, bf16[1,128,1024]{2,1,0:T(8,128)(2,1)} %gy_hbm.1, ...), custom_call_target="tpu_custom_call" | custom-call | flops 1000000000 | bytes 4000000 | tf_op jit(solution)/shard_map/pallas_call | solution.py:334
  79.5 1.0 %shard_map.113 = (bf16[1,128,1024]{2,1,0:T(8,128)(2,1)}, bf16[1,128,1024]{2,1,0:T(8,128)(2,1)}, f32[128,1024]{1,0:T(8,128)}) custom-call(bf16[1,128,1024]{2,1,0:T(8,128)(2,1)S(1)} %get-tuple-element.6.refs_0_, bf16[1,128,1024]{2,1,0:T(8,128)(2,1)S(1)} %get-tuple-element.7.refs_1_, f32[128,1024]{1,0:T(8,128)S(1)} %get-tuple-element.8.refs_2_), custom_call_target="tpu_custom_call" | custom-call | tf_op jit(solution)/shard_map/pallas_call | solution.py:357
